TPU v7x, 1024 devices: a whole 8x8x8 slice. The times are simulated.
1024 devices in a mesh: frame: 16 (over x, core), row: 8 (over z), expert: 8 (over y).
Axes of the slice: x: 8, y: 8, z: 8, core: 2. Of those that a mesh axis runs over, the one named last changes fastest.
Arguments:
- layer_input: bfloat16 [16, 8, 128, 2048], P('frame', 'row', None, 'expert'), may hold values from -6 to 6
- conv_out: bfloat16 [16, 8, 128, 2048], P('frame', 'row', None, 'expert'), may hold values from -6 to 6
- modulation: float32 [16, 8, 128, 2048], P('frame', 'row', None, 'expert'), may hold values from -6 to 6
- kernel: float32 [3, 3, 3, 2048], P(None, None, None, 'expert'), may hold values from -1.25 to 1.25
- out_grad: bfloat16 [16, 8, 128, 2048], P('frame', 'row', None, 'expert'), may hold values from -6 to 6
- routes: int32 [16, 8, 128, 2], P('frame', 'row'), may hold values from 0 to 15, all different within a row; in each aligned block of 128 rows (0 to 127, 128 to 255, ..., all dimensions but the last counted through in order) at most 17 rows name the same one
- gates: float32 [16, 8, 128, 2], P('frame', 'row'), may hold values from 0.1 to 1
- w_gate: bfloat16 [16, 2048, 6144], P('frame', None, 'expert'), may hold values from -0.125 to 0.125
- w_up: bfloat16 [16, 2048, 6144], P('frame', None, 'expert'), may hold values from -0.125 to 0.125
- w_down: bfloat16 [16, 6144, 2048], P('frame', 'expert'), may hold values from -0.078125 to 0.078125
Outputs:
- input_grad: float32 [16, 8, 128, 2048], P('frame', 'row', None, 'expert')
- mod_grad: float32 [16, 8, 128, 2048], P('frame', 'row', None, 'expert')
Inputs may be any that keep to these rules, and one draw needn't show every extreme that they name: The 2 routes of a token name different experts; of the routes of the 128 tokens of one frame and one row, at most 17 name any one expert, and exactly 17 name some expert.
All inputs are finite; a program needn't handle non-finite values.
Results may differ from a plain program's by a relative error of at most 0.0028.
Values may be sent and summed in bfloat16 or wider, within the bound.
A program may use at most 64 MiB of HBM per device.

v0:
```python
import jax
import jax.numpy as jnp
from jax import lax
from jax.sharding import PartitionSpec as P


def with_halo(block, sides, width):
    for axis, dim in sides:
        count = lax.axis_size(axis)
        forward = [(i, i + 1) for i in range(count - 1)]
        backward = [(target, source) for source, target in forward]
        low = lax.ppermute(
            lax.slice_in_dim(block, block.shape[dim] - width, None, axis=dim), axis, forward
        )
        high = lax.ppermute(lax.slice_in_dim(block, 0, width, axis=dim), axis, backward)
        block = jnp.concatenate([low, block, high], axis=dim)
    return block


def spread_back(start, padded, kernel, frames, rows, columns):
    result = start
    for a in range(3):
        for b in range(3):
            for c in range(3):
                result = (
                    result
                    + kernel[a, b, c]
                    * padded[2 - a : 2 - a + frames, 2 - b : 2 - b + rows, 2 - c : 2 - c + columns]
                )
    return result


def hidden_grads(h_gate, h_up, act_grad):
    squashed = jax.nn.sigmoid(h_gate)
    gate_grad = (act_grad * h_up * squashed * (1.0 + h_gate * (1.0 - squashed))).astype(
        jnp.bfloat16
    )
    up_grad = (act_grad * h_gate * squashed).astype(jnp.bfloat16)
    return (gate_grad, up_grad)


def shards(
    layer_input, conv_out, modulation, kernel, out_grad, routes, gates, w_gate, w_up, w_down
):
    columns = layer_input.shape[2]
    channels = layer_input.shape[3]
    local_experts = w_gate.shape[0]
    frame_count = lax.axis_size("frame")
    experts = local_experts * frame_count
    capacity = max(2, 2 * columns // experts + 1)
    tok_rows = layer_input.reshape(columns, channels)
    tok_grad = out_grad.reshape(columns, channels)
    route_ids = routes.reshape(columns, 2)
    gate_vals = gates.reshape(columns, 2)
    onehot = (route_ids[:, :, None] == jnp.arange(experts, dtype=jnp.int32)[None, None, :]).astype(
        jnp.int32
    )
    flat_hot = onehot.reshape(2 * columns, experts)
    earlier = jnp.cumsum(flat_hot, axis=0) - flat_hot
    rank_ids = jnp.sum(earlier * flat_hot, axis=1).reshape(columns, 2)
    slot_ids = route_ids * capacity + rank_ids
    placing = (
        slot_ids[:, :, None] == jnp.arange(experts * capacity, dtype=jnp.int32)[None, None, :]
    ).astype(jnp.bfloat16)
    send_rows = jnp.einsum(
        "tks,tc->sc", placing, tok_rows, preferred_element_type=jnp.float32
    ).astype(jnp.bfloat16)
    pair_grad = (gate_vals[:, :, None] * tok_grad[:, None, :].astype(jnp.float32)).astype(
        jnp.bfloat16
    )
    send_grad = jnp.einsum(
        "tks,tkc->sc", placing, pair_grad, preferred_element_type=jnp.float32
    ).astype(jnp.bfloat16)
    send_rows = send_rows.reshape(experts, capacity, channels)
    send_grad = send_grad.reshape(experts, capacity, channels)
    recv_rows, recv_grad = (
        lax.all_to_all(send_rows, "frame", split_axis=0, concat_axis=1, tiled=True),
        lax.all_to_all(send_grad, "frame", split_axis=0, concat_axis=1, tiled=True),
    )
    full_rows, full_grad = (
        lax.all_gather(recv_rows, "expert", axis=2, tiled=True),
        lax.all_gather(recv_grad, "expert", axis=2, tiled=True),
    )
    h_gate = jnp.einsum("esd,edh->esh", full_rows, w_gate, preferred_element_type=jnp.float32)
    h_up = jnp.einsum("esd,edh->esh", full_rows, w_up, preferred_element_type=jnp.float32)
    act_grad = jnp.einsum("esd,ehd->esh", full_grad, w_down, preferred_element_type=jnp.float32)
    gate_grad, up_grad = hidden_grads(h_gate, h_up, act_grad)
    terms = jnp.einsum("esh,edh->esd", gate_grad, w_gate, preferred_element_type=jnp.float32)
    terms = terms + jnp.einsum("esh,edh->esd", up_grad, w_up, preferred_element_type=jnp.float32)
    back = lax.psum_scatter(terms, "expert", scatter_dimension=2, tiled=True)
    returned = lax.all_to_all(
        back.astype(jnp.bfloat16), "frame", split_axis=1, concat_axis=0, tiled=True
    )
    flat_back = returned.reshape(experts * capacity, channels)
    moe_grad = jnp.einsum("tks,sc->tc", placing, flat_back, preferred_element_type=jnp.float32)
    total_grad = (tok_grad.astype(jnp.float32) + moe_grad).reshape(1, 1, columns, channels)
    weighted = modulation * total_grad
    padded = with_halo(weighted, (("frame", 0), ("row", 1)), 1)
    padded = jnp.pad(padded, ((0, 0), (0, 0), (1, 1), (0, 0)))
    input_grad = spread_back(total_grad, padded, kernel, 1, 1, columns)
    mod_grad = total_grad * conv_out.astype(jnp.float32)
    return (input_grad, mod_grad)


def solution(mesh):
    return jax.shard_map(
        shards,
        mesh=mesh,
        in_specs=(
            P("frame", "row", None, "expert"),
            P("frame", "row", None, "expert"),
            P("frame", "row", None, "expert"),
            P(None, None, None, "expert"),
            P("frame", "row", None, "expert"),
            P("frame", "row", None, None),
            P("frame", "row", None, None),
            P("frame", None, "expert"),
            P("frame", None, "expert"),
            P("frame", "expert", None),
        ),
        out_specs=(P("frame", "row", None, "expert"), P("frame", "row", None, "expert")),
        check_vma=False,
    )
```

profile of v0, /device:TPU:1, one launch (start us, length us, event | category | flops | bytes accessed | tf_op | source)
XLA Modules:
  0.0 248.5 jit_solution(526894061456189409)
XLA Ops:
  7.2 0.0 all-gather.5.cloned.1.call-start
  7.2 0.9 copy.23
  8.2 0.1 eq.43
  8.3 0.1 eq.39
  8.5 0.6 reduce-window.6
  9.1 0.2 slice_reduce_fusion
  9.3 0.1 fusion.76
  9.4 0.1 reshape.171
  9.5 0.1 copy.27
  9.6 0.1 convert_reduce_fusion
  9.7 0.6 copy-done.1
  10.3 1.0 convolution_convert_fusion
  11.3 0.1 reshape.176
  11.4 26.9 %all_to_all.33 = bf16[16,17,256]{2,1,0:T(8,128)(2,1)S(1)} all-to-all(bf16[16,17,256]{2,1,0:T(8,128)(2,1)S(1)} %reshape.176), channel_id=1, replica_groups=mesh['frame'=16,'row'=8,'expert'=8] {'frame'}, dimensions={0} | all-to-all | bytes 278528 | tf_op jit(solution)/shard_map/all_to_all | solution.py:77
  38.3 0.7 all_to_all.13
  39.1 0.0 all-gather.3.cloned.1.call-start
  39.1 0.9 bitcast_convert_fusion
  40.0 0.3 fusion.29
  40.3 0.1 reshape.172
  40.3 13.0 %all_to_all.34 = bf16[16,17,256]{2,1,0:T(8,128)(2,1)S(1)} all-to-all(bf16[16,17,256]{2,1,0:T(8,128)(2,1)S(1)} %reshape.172), channel_id=1, replica_groups=mesh['frame'=16,'row'=8,'expert'=8] {'frame'}, dimensions={0} | all-to-all | bytes 278528 | tf_op jit(solution)/shard_map/all_to_all | solution.py:78
  53.3 0.7 all_to_all.11
  54.0 0.0 all-gather.3.cloned.1.call-update
  54.0 0.0 reduce-scatter.2.cloned.1.call-start
  54.1 24.6 %all-gather.5.cloned.1.call-done = bf16[1,272,2048]{2,1,0:T(8,128)(2,1)} async-done(((bf16[1,272,256]{2,1,0:T(8,128)(2,1)}), bf16[1,272,2048]{2,1,0:T(8,128)(2,1)}) %all-gather.5.cloned.1.call-update) | async-done | bytes 1114128 | tf_op jit(solution)/shard_map/all_gather | solution.py:81
  78.7 4.2 %fusion.2 = f32[272,768]{1,0:T(8,128)} fusion(bf16[1,2048,768]{2,1,0:T(8,128)(2,1)} %param.17, bf16[1,272,2048]{2,1,0:T(8,128)(2,1)} %all-gather.5.cloned.1.call-done), kind=kOutput, calls=%fused_computation.2 | convolution fusion | flops 855638016 | bytes 5095424 | tf_op jit(solution)/shard_map/esd,edh->esh/dot_general | solution.py:84
  82.9 43.6 %all-gather.3.cloned.1.call-done = bf16[1,272,2048]{2,1,0:T(8,128)(2,1)} async-done(((bf16[1,272,256]{2,1,0:T(8,128)(2,1)}), bf16[1,272,2048]{2,1,0:T(8,128)(2,1)}) %all-gather.3.cloned.1.call-update) | async-done | bytes 1114128 | tf_op jit(solution)/shard_map/all_gather | solution.py:82
  126.6 4.2 %fusion.8 = f32[272,768]{1,0:T(8,128)} fusion(bf16[1,768,2048]{2,1,0:T(8,128)(2,1)} %param.19, bf16[1,272,2048]{2,1,0:T(8,128)(2,1)} %all-gather.3.cloned.1.call-done), kind=kOutput, calls=%fused_computation.8 | convolution fusion | flops 855638016 | bytes 5095424 | tf_op jit(solution)/shard_map/esd,ehd->esh/dot_general | solution.py:86
  130.8 6.4 %fusion = f32[272,2048]{1,0:T(8,128)} fusion(bf16[1,2048,768]{2,1,0:T(8,128)(2,1)} %param.17, f32[272,768]{1,0:T(8,128)} %fusion.8, bf16[1,2048,768]{2,1,0:T(8,128)(2,1)S(1)} %copy-done, bf16[1,272,2048]{2,1,0:T(8,128)(2,1)} %all-gather.5.cloned.1.call-done, f32[272,768]{1,0:T(8,128)} %fusion.2), kind=kOutput, calls=%fused_computation | convolution fusion | flops 1713364992 | bytes 11304960 | tf_op jit(solution)/shard_map/esh,edh->esd/dot_general | solution.py:88
  137.1 4.6 %fusion.13 = f32[1,272,2048]{2,1,0:T(8,128)} fusion(f32[272,2048]{1,0:T(8,128)} %fusion, bf16[1,2048,768]{2,1,0:T(8,128)(2,1)S(1)} %copy-done, f32[272,768]{1,0:T(8,128)} %fusion.8, f32[272,768]{1,0:T(8,128)} %fusion.2), kind=kOutput, calls=%fused_computation.11 | convolution fusion | flops 857448448 | bytes 9273344 | tf_op jit(solution)/shard_map/esh,edh->esd/dot_general | solution.py:89
  141.8 0.0 reduce-scatter.2.cloned.1.call-update
  141.8 48.0 %reduce-scatter.2.cloned.1.call-done = f32[1,272,256]{2,1,0:T(8,128)} async-done(((f32[1,272,2048]{2,1,0:T(8,128)}), f32[1,272,256]{2,1,0:T(8,128)}) %reduce-scatter.2.cloned.1.call-update) | async-done | bytes 278544 | tf_op jit(solution)/shard_map/reduce_scatter | solution.py:90
  189.8 1.0 convert_element_type.63
  190.7 0.2 copy.39
  190.9 0.5 broadcast.87
  191.5 2.1 reduce.2
  193.6 1.0 reshape.185
  194.6 20.5 %all_to_all.35 = bf16[16,2,2176]{2,1,0:T(2,128)(2,1)} all-to-all(bf16[16,2,2176]{2,1,0:T(2,128)(2,1)S(1)} %reshape.185), channel_id=1, replica_groups=mesh['frame'=16,'row'=8,'expert'=8] {'frame'}, dimensions={0} | all-to-all | bytes 278528 | tf_op jit(solution)/shard_map/all_to_all | solution.py:91
  215.1 1.4 reshape.186
  216.5 1.8 convert_multiply_fusion
  218.3 1.9 collective-permute-start
  220.2 2.4 collective-permute-start.1
  222.6 3.9 %collective-permute-done.1 = f32[1,1,128,256]{3,2,1,0:T(8,128)S(1)} collective-permute-done((f32[1,1,128,256]{3,2,1,0:T(8,128)S(1)}, f32[1,1,128,256]{3,2,1,0:T(8,128)S(1)}, u32[]{:S(2)}, u32[]{:S(2)}) %collective-permute-start.1) | collective-permute-done | bytes 131104 | tf_op jit(solution)/shard_map/ppermute | solution.py:15
  226.5 3.4 %collective-permute-start.2 = (f32[3,1,128,256]{3,2,1,0:T(8,128)S(1)}, f32[3,1,128,256]{3,2,1,0:T(8,128)S(1)}, u32[]{:S(2)}, u32[]{:S(2)}) collective-permute-start(f32[3,1,128,256]{3,2,1,0:T(8,128)S(1)} %pad_maximum_fusion), channel_id=1, source_target_pairs={{0,8},{8,16},{16,24},{24,32},{32,40},{40,48},{48,56},{1,9},{9,17},... | collective-permute-start | bytes 1179656 | tf_op jit(solution)/shard_map/ppermute | solution.py:12
  229.9 1.3 collective-permute-start.3
  231.2 5.5 %collective-permute-done.2 = f32[3,1,128,256]{3,2,1,0:T(8,128)S(1)} collective-permute-done((f32[3,1,128,256]{3,2,1,0:T(8,128)S(1)}, f32[3,1,128,256]{3,2,1,0:T(8,128)S(1)}, u32[]{:S(2)}, u32[]{:S(2)}) %collective-permute-start.2) | collective-permute-done | bytes 393248 | tf_op jit(solution)/shard_map/ppermute | solution.py:12
  236.7 4.1 %collective-permute-done.3 = f32[3,1,128,256]{3,2,1,0:T(8,128)S(1)} collective-permute-done((f32[3,1,128,256]{3,2,1,0:T(8,128)S(1)}, f32[3,1,128,256]{3,2,1,0:T(8,128)S(1)}, u32[]{:S(2)}, u32[]{:S(2)}) %collective-permute-start.3) | collective-permute-done | bytes 393248 | tf_op jit(solution)/shard_map/ppermute | solution.py:15
  240.8 0.1 select_maximum_fusion
  241.0 1.0 fusion.44
  (18 shorter events, 0.2 us)
Async XLA Ops:
  7.2 123.6 %copy-start = (bf16[1,2048,768]{2,1,0:T(8,128)(2,1)S(1)}, bf16[1,2048,768]{2,1,0:T(8,128)(2,1)}, u32[]{:S(2)}) copy-start(bf16[1,2048,768]{2,1,0:T(8,128)(2,1)} %param.18) | copy-start | bytes 9437188
  7.2 32.8 %copy-start.4 = (f32[1,1,128,2]{2,3,1,0:T(2,128)S(1)}, f32[1,1,128,2]{2,3,1,0:T(2,128)}, u32[]{:S(2)}) copy-start(f32[1,1,128,2]{2,3,1,0:T(2,128)} %param.16) | copy-start | bytes 3076
  7.2 71.5 %all-gather.5.cloned.1.call-start = ((), (), s32[]{:S(2)}) async-start(), calls=%async_computation.5 | async-start | bytes 1253376 | tf_op jit(solution)/shard_map/all_gather | solution.py:81
  9.7 0.6 copy-start.1
  39.1 87.5 %all-gather.3.cloned.1.call-start = ((), (), s32[]{:S(2)}) async-start(), calls=%async_computation.4 | async-start | bytes 1253376 | tf_op jit(solution)/shard_map/all_gather | solution.py:82
  54.0 135.7 %reduce-scatter.2.cloned.1.call-start = ((), (), s32[]{:S(2)}) async-start(), calls=%async_computation.6 | async-start | bytes 2506752 | tf_op jit(solution)/shard_map/reduce_scatter | solution.py:90
  141.8 74.7 %copy-start.2 = (bf16[128,272]{0,1:T(8,128)(2,1)S(1)}, bf16[128,272]{0,1:T(8,128)(2,1)}, u32[]{:S(2)}) copy-start(bf16[128,272]{0,1:T(8,128)(2,1)} %copy-done.1) | copy-start | bytes 208900
  193.6 37.6 %copy-start.3 = (f32[3,3,3,256]{3,2,1,0:T(4,128)S(1)}, f32[3,3,3,256]{3,2,1,0:T(4,128)}, u32[]{:S(2)}) copy-start(f32[3,3,3,256]{3,2,1,0:T(4,128)} %param.13) | copy-start | bytes 82948
  218.3 4.3 %collective-permute-start = (f32[1,1,128,256]{3,2,1,0:T(8,128)S(1)}, f32[1,1,128,256]{3,2,1,0:T(8,128)S(1)}, u32[]{:S(2)}, u32[]{:S(2)}) collective-permute-start(f32[1,1,128,256]{3,2,1,0:T(8,128)S(1)} %get-tuple-element.3), channel_id=1, source_target_pairs={{0,64},{64,128},{128,192},{192,256},{256,320},{320,384},{384,448},... | collective-permute-start | bytes 393224 | tf_op jit(solution)/shard_map/ppermute | solution.py:12
  220.2 6.3 %collective-permute-start.1 = (f32[1,1,128,256]{3,2,1,0:T(8,128)S(1)}, f32[1,1,128,256]{3,2,1,0:T(8,128)S(1)}, u32[]{:S(2)}, u32[]{:S(2)}) collective-permute-start(f32[1,1,128,256]{3,2,1,0:T(8,128)S(1)} %get-tuple-element.3), channel_id=1, source_target_pairs={{64,0},{128,64},{192,128},{256,192},{320,256},{384,320},{448,384},... | collective-permute-start | bytes 393224 | tf_op jit(solution)/shard_map/ppermute | solution.py:15
  226.5 10.2 %collective-permute-start.2 = (f32[3,1,128,256]{3,2,1,0:T(8,128)S(1)}, f32[3,1,128,256]{3,2,1,0:T(8,128)S(1)}, u32[]{:S(2)}, u32[]{:S(2)}) collective-permute-start(f32[3,1,128,256]{3,2,1,0:T(8,128)S(1)} %pad_maximum_fusion), channel_id=1, source_target_pairs={{0,8},{8,16},{16,24},{24,32},{32,40},{40,48},{48,56},{1,9},{9,17},... | collective-permute-start | bytes 1179656 | tf_op jit(solution)/shard_map/ppermute | solution.py:12
  229.9 10.9 %collective-permute-start.3 = (f32[3,1,128,256]{3,2,1,0:T(8,128)S(1)}, f32[3,1,128,256]{3,2,1,0:T(8,128)S(1)}, u32[]{:S(2)}, u32[]{:S(2)}) collective-permute-start(f32[3,1,128,256]{3,2,1,0:T(8,128)S(1)} %pad_maximum_fusion), channel_id=1, source_target_pairs={{8,0},{16,8},{24,16},{32,24},{40,32},{48,40},{56,48},{9,1},{17,9},... | collective-permute-start | bytes 1179656 | tf_op jit(solution)/shard_map/ppermute | solution.py:15
Sparse Core Ops, SparseCore 0:
  39.2 39.4 all-gather.4
  81.3 45.2 all-gather.2
  141.9 47.8 reduce-scatter.1
where the time goes:
time: 249 us
  waiting for transfers between devices  130 us (52%)
  blocking collectives  60.4 us (24%)
  matrix products  22.5 us (9%)
  between operations  14 us (6%)
  starting transfers between devices  9.09 us (4%)
  local copies, waits for them, and re-layouts  6.9 us (3%)
  other arithmetic  5.94 us (2%)
    reduce_scatter x1, waiting for transfers between devices, shards(): back = lax.psum_scatter(terms, 'expert', scatter_dimension=2, tiled=True)  48 us
    all_gather x1, waiting for transfers between devices, shards(): lax.all_gather(recv_grad, 'expert', axis=2, tiled=True)  43.6 us
    all_to_all x1, blocking collectives, shards(): lax.all_to_all(send_rows, 'frame', split_axis=0, concat_axis=1, tiled=True)  26.9 us
    all_gather x1, waiting for transfers between devices, shards(): lax.all_gather(recv_rows, 'expert', axis=2, tiled=True)  24.6 us
    all_to_all x1, blocking collectives, shards(): lax.all_to_all(back.astype(jnp.bfloat16), 'frame', split_axis=1, concat_a...  20.5 us
    all_to_all x1, blocking collectives, shards(): lax.all_to_all(send_grad, 'frame', split_axis=0, concat_axis=1, tiled=True)  13 us
    ppermute x2, waiting for transfers between devices, with_halo(): lax.ppermute(lax.slice_in_dim(block, 0, width, axis=dim), axis, backward)  7.98 us
    dot_general x1, matrix products, shards(): jnp.einsum('esh,edh->esd', gate_grad, w_gate, preferred_element_type=jnp....  6.39 us
  transfers between devices with their start and end apart: 7, of which 6 were waited for; matrix products, arithmetic and copies ran while one was open for 2% of the time, Pallas kernels for 0%

commit v1 on v0

v1 whole, which is shorter than its diff:
```python
import functools

import jax
import jax.numpy as jnp
from jax import lax
from jax.experimental import pallas as pl
from jax.experimental.pallas import tpu as pltpu
from jax.sharding import PartitionSpec as P

MESH = pl.DeviceIdType.MESH
BF16 = jnp.bfloat16
F32 = jnp.float32
LANE = 128
RANKS = 16


def hidden_grads(h_gate, h_up, act_grad):
    squashed = jax.nn.sigmoid(h_gate)
    gate_grad = act_grad * h_up * squashed * (1.0 + h_gate * (1.0 - squashed))
    up_grad = act_grad * h_gate * squashed
    return gate_grad.astype(BF16), up_grad.astype(BF16)


def dot_nn(a, b):
    return lax.dot_general(a, b, (((1,), (0,)), ((), ())), preferred_element_type=F32)


def dot_nt(a, b):
    return lax.dot_general(a, b, (((1,), (1,)), ((), ())), preferred_element_type=F32)


def dot_tn(a, b):
    return lax.dot_general(a, b, (((0,), (0,)), ((), ())), preferred_element_type=F32)


def body(
    frames,
    rows,
    experts,
    split,
    li_hbm,
    co_hbm,
    mo_hbm,
    ke_hbm,
    og_hbm,
    ro_hbm,
    ga_hbm,
    wg_hbm,
    wu_hbm,
    wd_hbm,
    ig_hbm,
    mg_hbm,
    li,
    co,
    mo,
    ke,
    og,
    ro,
    ga,
    wg,
    wu,
    wd,
    in_sem,
    pt,
    send,
    esend,
    erecv,
    gbuf,
    hg,
    hu,
    ag,
    gg,
    ug,
    term,
    rs_send,
    rs_recv,
    bsend,
    besend,
    bk,
    berecv,
    wbuf,
    usend,
    urecv,
    igv,
    mgv,
    out_sem,
    xs_sem,
    xr_sem,
    as_sem,
    ar_sem,
    rs_ssem,
    rs_rsem,
    bs_sem,
    br_sem,
    hs_sem,
    hr_sem,
    us_sem,
    ur_sem,
):
    tokens, chan = li.shape
    half = experts // 2
    main = frames * RANKS
    slots = gg.shape[0]
    f = lax.axis_index("frame")
    r = lax.axis_index("row")
    y = lax.axis_index("expert")
    right = lax.rem(y + 1, experts)
    left = lax.rem(y + experts - 1, experts)

    loads = [
        pltpu.make_async_copy(src, dst, in_sem.at[i])
        for i, (src, dst) in enumerate(
            [
                (ro_hbm, ro),
                (ga_hbm, ga),
                (li_hbm, li),
                (og_hbm, og),
                (wg_hbm, wg),
                (wu_hbm, wu),
                (wd_hbm, wd),
                (co_hbm, co),
                (mo_hbm, mo),
                (ke_hbm, ke),
            ]
        )
    ]
    for load in loads:
        load.start()

    barrier = pltpu.get_barrier_semaphore()

    def greet(off, carry):
        pl.semaphore_signal(
            barrier, inc=1, device_id={"frame": lax.rem(f + off, frames)}, device_id_type=MESH
        )
        return carry

    lax.fori_loop(1, frames, greet, 0)
    pl.semaphore_signal(barrier, inc=1, device_id={"expert": right}, device_id_type=MESH)
    pl.semaphore_signal(barrier, inc=1, device_id={"expert": left}, device_id_type=MESH)

    for step in (1, rows - 1):
        pl.semaphore_signal(
            barrier, inc=1, device_id={"row": lax.rem(r + step, rows)}, device_id_type=MESH
        )

    for load in loads[:4]:
        load.wait()
    ids0, ids1 = ro[0:1, :], ro[1:2, :]
    iota_e = lax.broadcasted_iota(jnp.int32, (frames, tokens), 0)
    hot0, hot1 = iota_e == ids0, iota_e == ids1
    hot = jnp.where(hot0 | hot1, 1.0, 0.0).astype(BF16)
    before = (
        lax.broadcasted_iota(jnp.int32, (tokens, tokens), 0)
        < lax.broadcasted_iota(jnp.int32, (tokens, tokens), 1)
    )
    earlier = dot_nn(hot, jnp.where(before, 1.0, 0.0).astype(BF16))
    rank0 = jnp.sum(jnp.where(hot0, earlier, 0.0), axis=0, keepdims=True).astype(jnp.int32)
    rank1 = jnp.sum(jnp.where(hot1, earlier, 0.0), axis=0, keepdims=True).astype(jnp.int32)
    slot0 = jnp.where(rank0 < RANKS, ids0 * RANKS + rank0, main + ids0)
    slot1 = jnp.where(rank1 < RANKS, ids1 * RANKS + rank1, main + ids1)
    iota_s = lax.broadcasted_iota(jnp.int32, (slots, tokens), 0)
    at0, at1 = iota_s == slot0, iota_s == slot1
    slot_gate = jnp.sum(
        jnp.where(at0, ga[0:1, :], 0.0) + jnp.where(at1, ga[1:2, :], 0.0), axis=1, keepdims=True
    )
    pt[...] = jnp.where(at0 | at1, 1.0, 0.0).astype(BF16)

    xs = dot_nn(pt[...], li[...])
    gs = (dot_nn(pt[...], og[...]) * slot_gate).astype(BF16)
    send[0] = xs[:main].astype(BF16)
    send[1] = gs[:main]
    extra = [xs[main:], gs[main:].astype(F32)]
    for j in range(4):
        esend[pl.ds(j, frames, stride=8), :] = extra[j // 2][
            :frames, (j % 2) * LANE : (j % 2 + 1) * LANE
        ]

    pl.semaphore_wait(barrier, frames - 1 + 2 + 2)

    def tile(index, size):
        return pl.ds(pl.multiple_of(index * size, size), size)

    def dispatch(to, at, kind, sems):
        if kind == 2:
            src, dst = esend.at[tile(to, 8)], erecv.at[tile(at, 8)]
        else:
            src, dst = send.at[kind, tile(to, RANKS)], gbuf.at[y, kind, tile(at, RANKS)]
        return pltpu.make_async_remote_copy(
            src_ref=src,
            dst_ref=dst,
            send_sem=xs_sem.at[kind, sems],
            recv_sem=xr_sem.at[kind, at],
            device_id={"frame": to},
            device_id_type=MESH,
        )

    def dispatch_x(off, carry):
        to = lax.rem(f + off, frames)
        dispatch(to, f, 0, to).start()
        dispatch(to, f, 2, to).start()
        return carry

    def dispatch_g(off, carry):
        to = lax.rem(f + off, frames)
        dispatch(to, f, 1, to).start()
        return carry

    lax.fori_loop(1, frames, dispatch_x, 0)
    lax.fori_loop(1, frames, dispatch_g, 0)
    for kind in range(2):
        gbuf[y, kind, tile(f, RANKS), :] = send[kind, tile(f, RANKS), :]
    erecv[tile(f, 8), :] = esend[tile(f, 8), :]

    def arrived(kinds):
        def step(off, carry):
            at = lax.rem(f + off, frames)
            for kind in kinds:
                dispatch(at, at, kind, at).wait_recv()
            return carry

        lax.fori_loop(1, frames, step, 0)

    def unpack_extra(kind):
        pieces = [erecv[pl.ds(2 * kind + j, frames, stride=8), :] for j in range(2)]
        value = jnp.concatenate(pieces, axis=1)
        if slots - main > frames:
            value = jnp.concatenate(
                [value, jnp.zeros((slots - main - frames, chan), F32)], axis=0
            )
        gbuf[y, kind, main:slots, :] = value.astype(BF16)

    def gather(way, dist, kind):
        owner = lax.rem(y + (experts - dist if way == 0 else dist), experts)
        return pltpu.make_async_remote_copy(
            src_ref=gbuf.at[owner, kind],
            dst_ref=gbuf.at[owner, kind],
            send_sem=as_sem.at[way, dist, kind],
            recv_sem=ar_sem.at[way, dist, kind],
            device_id={"expert": right if way == 0 else left},
            device_id_type=MESH,
        )

    def columns(owner):
        return pl.ds(pl.multiple_of(owner * chan, chan), chan)

    def add_block(owner, kind, first):
        block = gbuf[owner, kind]
        for n in range(0, hg.shape[1], chan):
            cut = slice(n, n + chan)
            if kind == 0:
                for acc, w in ((hg, wg), (hu, wu)):
                    value = dot_nn(block, w[columns(owner), cut])
                    acc[:, cut] = value if first else acc[:, cut] + value
            else:
                value = dot_nt(block, wd[cut, columns(owner)])
                ag[:, cut] = value if first else ag[:, cut] + value

    arrived((0, 2))
    unpack_extra(0)
    for way in range(2):
        gather(way, 0, 0).start()
    loads[4].wait()
    loads[5].wait()
    add_block(y, 0, True)
    arrived((1,))
    unpack_extra(1)
    for way in range(2):
        gather(way, 0, 1).start()
    loads[6].wait()
    add_block(y, 1, True)

    def owner_of(way, dist):
        return lax.rem(y + (experts - dist if way == 0 else dist), experts)

    def ring(dist):
        for kind in range(2):
            for way in range(2):
                gather(way, dist - 1, kind).wait_recv()
                if isinstance(dist, int) and dist == half - 1:
                    if kind == way:
                        gather(way, dist, kind).start()
                else:
                    gather(way, dist, kind).start()
            for way in range(2):
                add_block(owner_of(way, dist), kind, False)

    if half > 2:

        def ring_step(dist, carry):
            ring(dist)
            return carry

        lax.fori_loop(1, half - 1, ring_step, 0)
    ring(half - 1)
    for way in range(2):
        gather(way, half - 1, way).wait_recv()
        add_block(owner_of(way, half), way, False)

    def hidden(i, carry):
        at = tile(i, 16)
        gg[at, :], ug[at, :] = hidden_grads(hg[at, :], hu[at, :], ag[at, :])
        return carry

    lax.fori_loop(0, slots // 16, hidden, 0)

    parts = (slice(0, split), slice(split, slots))

    def make_term(owner):
        at = columns(owner)
        return dot_nt(gg[...], wg[at, :]) + dot_nt(ug[...], wu[at, :])

    def reduce_copy(way, step, part):
        return pltpu.make_async_remote_copy(
            src_ref=rs_send.at[way, step, parts[part]],
            dst_ref=rs_recv.at[way, step, parts[part]],
            send_sem=rs_ssem.at[way, step, part],
            recv_sem=rs_rsem.at[way, step, part],
            device_id={"expert": right if way == 0 else left},
            device_id_type=MESH,
        )

    term[0] = make_term(lax.rem(y + half, experts))
    for way in range(2):
        rs_send[way, 0, parts[way]] = term[0, parts[way]].astype(BF16)
        reduce_copy(way, 0, way).start()

    def reduce_step(step):
        for way in range(2):
            term[way] = make_term(
                lax.rem(y + (half - step if way == 0 else experts - half + step), experts)
            )
        for late in range(2):
            for way in range(2):
                part = way if late else 1 - way
                value = term[way, parts[part]]
                if late or not (isinstance(step, int) and step == 1):
                    reduce_copy(way, step - 1, part).wait_recv()
                    value = value + rs_recv[way, step - 1, parts[part]].astype(F32)
                rs_send[way, step, parts[part]] = value.astype(BF16)
                reduce_copy(way, step, part).start()

    reduce_step(1)
    if half > 2:

        def reduce_loop(step, carry):
            reduce_step(step)
            return carry

        lax.fori_loop(2, half, reduce_loop, 0)
    term[0] = make_term(y)
    for part in range(2):
        for way in range(2):
            reduce_copy(way, half - 1, part).wait_recv()
        term[1, parts[part]] = (
            term[0, parts[part]]
            + rs_recv[0, half - 1, parts[part]].astype(F32)
            + rs_recv[1, half - 1, parts[part]].astype(F32)
        )
    bsend[...] = term[1, 0:main].astype(BF16)
    back_extra = term[1, main:slots].astype(BF16).astype(F32)
    for j in range(2):
        besend[pl.ds(j, frames, stride=8), :] = back_extra[:frames, j * LANE : (j + 1) * LANE]

    def give_back(to, at, kind, sems):
        size = (RANKS, 8)[kind]
        src, dst = ((bsend, bk), (besend, berecv))[kind]
        return pltpu.make_async_remote_copy(
            src_ref=src.at[tile(to, size)],
            dst_ref=dst.at[tile(at, size)],
            send_sem=bs_sem.at[kind, sems],
            recv_sem=br_sem.at[kind, at],
            device_id={"frame": to},
            device_id_type=MESH,
        )

    def give_step(off, carry):
        to = lax.rem(f + off, frames)
        for kind in range(2):
            give_back(to, f, kind, to).start()
        return carry

    lax.fori_loop(1, frames, give_step, 0)
    bk[tile(f, RANKS), :] = bsend[tile(f, RANKS), :]
    berecv[tile(f, 8), :] = besend[tile(f, 8), :]
    for load in loads[7:]:
        load.wait()

    for i in range(3):
        wbuf[i, 0:8, :] = jnp.zeros((8, chan), F32)
        wbuf[i, 8 + tokens : 16 + tokens, :] = jnp.zeros((8, chan), F32)

    @pl.when(f == 0)
    def _():
        wbuf[0, 8 : 8 + tokens, :] = jnp.zeros((tokens, chan), F32)

    @pl.when(f == frames - 1)
    def _():
        wbuf[2, 8 : 8 + tokens, :] = jnp.zeros((tokens, chan), F32)

    def take_step(off, carry):
        at = lax.rem(f + off, frames)
        for kind in range(2):
            give_back(at, at, kind, at).wait_recv()
        return carry

    lax.fori_loop(1, frames, take_step, 0)
    pieces = [berecv[pl.ds(j, frames, stride=8), :] for j in range(2)]
    returned_extra = jnp.concatenate(pieces, axis=1).astype(BF16)
    total = (
        og[...].astype(F32)
        + dot_tn(pt[0:main, :], bk[...])
        + dot_tn(pt[main : main + frames, :], returned_extra)
    )
    igv[...] = total
    wbuf[1, 8 : 8 + tokens, :] = mo[...] * total

    inner = pl.ds(8, tokens)

    def frame_copy(way):
        return pltpu.make_async_remote_copy(
            src_ref=wbuf.at[1, inner],
            dst_ref=wbuf.at[0 if way == 0 else 2, inner],
            send_sem=hs_sem.at[way],
            recv_sem=hr_sem.at[way],
            device_id={"frame": f + 1 if way == 0 else f - 1},
            device_id_type=MESH,
        )

    @pl.when(f < frames - 1)
    def _():
        frame_copy(0).start()

    @pl.when(f > 0)
    def _():
        frame_copy(1).start()

    mgv[...] = total * co[...].astype(F32)
    mg_out = pltpu.make_async_copy(mgv, mg_hbm, out_sem.at[0])
    mg_out.start()

    chunk = 32

    def spread(b, a, at):
        value = None
        for c in range(3):
            start = 9 - c + at
            tap = ke[a, b, c : c + 1, :] * wbuf[2 - a, start : start + chunk, :]
            value = tap if value is None else value + tap
        return value

    places = (0, None, 1)
    for at in range(0, tokens, chunk):
        here = slice(at, at + chunk)
        igv[here, :] += spread(1, 1, at)
        for b in (0, 2):
            usend[places[b], here, :] = spread(b, 1, at)

    @pl.when(f > 0)
    def _():
        frame_copy(0).wait_recv()

    @pl.when(f < frames - 1)
    def _():
        frame_copy(1).wait_recv()

    for b in (0, 2):
        for at in range(0, tokens, chunk):
            here = slice(at, at + chunk)
            usend[places[b], here, :] += spread(b, 0, at) + spread(b, 2, at)

    def row_copy(way):
        return pltpu.make_async_remote_copy(
            src_ref=usend.at[way],
            dst_ref=urecv.at[way],
            send_sem=us_sem.at[way],
            recv_sem=ur_sem.at[way],
            device_id={"row": r - 1 if way == 0 else r + 1},
            device_id_type=MESH,
        )

    @pl.when(r > 0)
    def _():
        row_copy(0).start()

    @pl.when(r < rows - 1)
    def _():
        row_copy(1).start()

    for at in range(0, tokens, chunk):
        igv[at : at + chunk, :] += spread(1, 0, at) + spread(1, 2, at)

    @pl.when(r < rows - 1)
    def _():
        row_copy(0).wait_recv()
        igv[...] += urecv[0]

    @pl.when(r > 0)
    def _():
        row_copy(1).wait_recv()
        igv[...] += urecv[1]

    ig_out = pltpu.make_async_copy(igv, ig_hbm, out_sem.at[1])
    ig_out.start()

    def sent(off, carry):
        to = lax.rem(f + off, frames)
        for kind in range(3):
            dispatch(to, f, kind, to).wait_send()
        for kind in range(2):
            give_back(to, f, kind, to).wait_send()
        return carry

    lax.fori_loop(1, frames, sent, 0)
    for way in range(2):
        for dist in range(half):
            for kind in range(2):
                if dist < half - 1 or kind == way:
                    gather(way, dist, kind).wait_send()
        for step in range(half):
            for part in range(2):
                if step > 0 or part == way:
                    reduce_copy(way, step, part).wait_send()

    @pl.when(f < frames - 1)
    def _():
        frame_copy(0).wait_send()

    @pl.when(f > 0)
    def _():
        frame_copy(1).wait_send()

    @pl.when(r > 0)
    def _():
        row_copy(0).wait_send()

    @pl.when(r < rows - 1)
    def _():
        row_copy(1).wait_send()

    mg_out.wait()
    ig_out.wait()


def shards(
    layer_input, conv_out, modulation, kernel, out_grad, routes, gates, w_gate, w_up, w_down
):
    tokens, chan = layer_input.shape[2:]
    width, hidden = w_gate.shape[1:]
    frames, rows, experts = (lax.axis_size(a) for a in ("frame", "row", "expert"))
    assert w_gate.shape[0] == 1 and 2 * tokens == RANKS * frames and chan == 2 * LANE
    main = frames * RANKS
    slots = main + -(-frames // 16) * 16
    split = (slots // 16 + 1) // 2 * 16
    half = experts // 2
    vmem = pltpu.VMEM
    dma = pltpu.SemaphoreType.DMA
    scratch = [
        vmem((tokens, chan), BF16),
        vmem((tokens, chan), BF16),
        vmem((tokens, chan), F32),
        vmem((3, 3, 3, chan), F32),
        vmem((tokens, chan), BF16),
        vmem((2, tokens), jnp.int32),
        vmem((2, tokens), F32),
        vmem((width, hidden), BF16),
        vmem((width, hidden), BF16),
        vmem((hidden, width), BF16),
        dma((10,)),
        vmem((slots, tokens), BF16),
        vmem((2, main, chan), BF16),
        vmem((frames * 8, LANE), F32),
        vmem((frames * 8, LANE), F32),
        vmem((experts, 2, slots, chan), BF16),
        vmem((slots, hidden), F32),
        vmem((slots, hidden), F32),
        vmem((slots, hidden), F32),
        vmem((slots, hidden), BF16),
        vmem((slots, hidden), BF16),
        vmem((2, slots, chan), F32),
        vmem((2, half, slots, chan), BF16),
        vmem((2, half, slots, chan), BF16),
        vmem((main, chan), BF16),
        vmem((frames * 8, LANE), F32),
        vmem((main, chan), BF16),
        vmem((frames * 8, LANE), F32),
        vmem((3, tokens + 16, chan), F32),
        vmem((2, tokens, chan), F32),
        vmem((2, tokens, chan), F32),
        vmem((tokens, chan), F32),
        vmem((tokens, chan), F32),
        dma((2,)),
        dma((3, frames)),
        dma((3, frames)),
        dma((2, half, 2)),
        dma((2, half, 2)),
        dma((2, half, 2)),
        dma((2, half, 2)),
        dma((2, frames)),
        dma((2, frames)),
        dma((2,)),
        dma((2,)),
        dma((2,)),
        dma((2,)),
    ]
    out = jax.ShapeDtypeStruct((tokens, chan), F32)
    slot_flops = 2 * slots * width * hidden
    input_grad, mod_grad = pl.pallas_call(
        functools.partial(body, frames, rows, experts, split),
        out_shape=(out, out),
        in_specs=[pl.BlockSpec(memory_space=pl.ANY)] * 10,
        out_specs=(pl.BlockSpec(memory_space=pl.ANY),) * 2,
        scratch_shapes=scratch,
        compiler_params=pltpu.CompilerParams(
            collective_id=0, has_side_effects=True, vmem_limit_bytes=60 * 2**20
        ),
        cost_estimate=pl.CostEstimate(
            flops=5 * slot_flops,
            bytes_accessed=3 * 2 * width * hidden,
            transcendentals=slots * hidden,
        ),
        name="expert_backward",
    )(
        layer_input.reshape(tokens, chan),
        conv_out.reshape(tokens, chan),
        modulation.reshape(tokens, chan),
        kernel,
        out_grad.reshape(tokens, chan),
        routes.reshape(tokens, 2).T,
        gates.reshape(tokens, 2).T,
        w_gate.reshape(width, hidden),
        w_up.reshape(width, hidden),
        w_down.reshape(hidden, width),
    )
    shape = (1, 1, tokens, chan)
    return input_grad.reshape(shape), mod_grad.reshape(shape)


def solution(mesh):
    token = P("frame", "row", None, "expert")
    route = P("frame", "row", None, None)
    return jax.shard_map(
        shards,
        mesh=mesh,
        in_specs=(
            token,
            token,
            token,
            P(None, None, None, "expert"),
            token,
            route,
            route,
            P("frame", None, "expert"),
            P("frame", None, "expert"),
            P("frame", "expert", None),
        ),
        out_specs=(token, token),
        check_vma=False,
    )
```

time: 249 us -> 90.1 us (0.36)
  waiting for transfers between devices: 130 us -> 0 us
  Pallas kernels: 0 us -> 85.7 us
  blocking collectives: 60.4 us -> 0 us
  matrix products: 22.5 us -> 0 us
  between operations: 14 us -> 0.64 us
  starting transfers between devices: 9.09 us -> 0 us
  other arithmetic: 5.94 us -> 0 us
  local copies, waits for them, and re-layouts: 6.9 us -> 3.14 us
    pallas_call x0 -> x1, Pallas kernels: none -> 85.7 us  [shards(): pl.pallas_call(functools.partial(body, frames, rows, experts, split), out...]
    all_gather x2 -> x0, waiting for transfers between devices: 68.3 us -> none  [the longest x1 43.6 us: shards(): lax.all_gather(recv_grad, 'expert', axis=2, tiled=True)]
    all_to_all x3 -> x0, blocking collectives: 60.4 us -> none  [the longest x1 26.9 us: shards(): lax.all_to_all(send_rows, 'frame', split_axis=0, concat_axis=1, tiled=True)]
    reduce_scatter x1 -> x0, waiting for transfers between devices: 48 us -> none  [shards(): back = lax.psum_scatter(terms, 'expert', scatter_dimension=2, tiled=True)]
    dot_general x7 -> x0, matrix products: 22.5 us -> none  [the longest x1 6.39 us: shards(): jnp.einsum('esh,edh->esd', gate_grad, w_gate, preferred_element_type=jnp....]
    ppermute x4 -> x0, waiting for transfers between devices: 13.4 us -> none  [the longest x2 7.98 us: with_halo(): lax.ppermute(lax.slice_in_dim(block, 0, width, axis=dim), axis, backward)]
    ppermute x4 -> x0, starting transfers between devices: 8.97 us -> none  [the longest x2 5.26 us: with_halo(): lax.ppermute(lax.slice_in_dim(block, block.shape[dim] - width, None, axis...]
  transfers between devices with their start and end apart: 7 -> 0, of which waited for: 6 -> 0; matrix products, arithmetic and copies ran while one was open for 2% -> 0% of each run, Pallas kernels for 0% -> 0%
where the time goes in v1:
time: 90.1 us; the launch traced here: 89.5 us
  Pallas kernels  85.7 us (95%)
  local copies, waits for them, and re-layouts  3.14 us (3%)
    pallas_call x1, Pallas kernels, shards(): pl.pallas_call(functools.partial(body, frames, rows, experts, split), out...  85.7 us
    unnamed x2, local copies, waits for them, and re-layouts  3.14 us

profile of v1, /device:TPU:1, one launch (start us, length us, event | category | flops | bytes accessed | tf_op | source)
XLA Modules:
  0.0 89.5 jit_solution(15218386458102336096)
XLA Ops:
  0.6 85.7 %expert_backward.1 = (f32[128,256]{1,0:T(8,128)}, f32[128,256]{1,0:T(8,128)}) custom-call(bf16[128,256]{1,0:T(8,128)(2,1)} %bitcast.21, bf16[128,256]{1,0:T(8,128)(2,1)} %bitcast.22, f32[128,256]{1,0:T(8,128)} %bitcast.20, f32[3,3,3,256]{3,2,1,0:T(4,128)} %ke_hbm.1, bf16[128,256]{1,0:T(8,128)(2,1)} %bitcast.23, s32[2,128]{1,0:T(2,128)} %bitcast.24, ...), custom_call_target="tpu_custom_call" | custom-call | flops 4278190080 | bytes 9437184 | tf_op jit(solution)/shard_map/expert_backward/pallas_call | solution.py:608
  86.3 1.6 %copy.14 = f32[1,1,128,256]{3,2,1,0:T(8,128)} copy(f32[1,1,128,256]{3,2,1,0:T(8,128)} %bitcast.16) | data formatting | bytes 262144
  87.9 1.6 %copy.15 = f32[1,1,128,256]{3,2,1,0:T(8,128)} copy(f32[1,1,128,256]{3,2,1,0:T(8,128)} %bitcast.15) | data formatting | bytes 262144

commit v2 on v1

--- a/solution.py
+++ b/solution.py
@@ -39,7 +39,6 @@
     experts,
     split,
     li_hbm,
-    co_hbm,
     mo_hbm,
     ke_hbm,
     og_hbm,
@@ -48,10 +47,9 @@
     wg_hbm,
     wu_hbm,
     wd_hbm,
-    ig_hbm,
-    mg_hbm,
+    totv,
+    convv,
     li,
-    co,
     mo,
     ke,
     og,
@@ -81,9 +79,6 @@
     wbuf,
     usend,
     urecv,
-    igv,
-    mgv,
-    out_sem,
     xs_sem,
     xr_sem,
     as_sem,
@@ -118,7 +113,6 @@
                 (wg_hbm, wg),
                 (wu_hbm, wu),
                 (wd_hbm, wd),
-                (co_hbm, co),
                 (mo_hbm, mo),
                 (ke_hbm, ke),
             ]
@@ -172,9 +166,7 @@
     send[1] = gs[:main]
     extra = [xs[main:], gs[main:].astype(F32)]
     for j in range(4):
-        esend[pl.ds(j, frames, stride=8), :] = extra[j // 2][
-            :frames, (j % 2) * LANE : (j % 2 + 1) * LANE
-        ]
+        esend[:, j, :] = extra[j // 2][:frames, (j % 2) * LANE : (j % 2 + 1) * LANE]
 
     pl.semaphore_wait(barrier, frames - 1 + 2 + 2)
 
@@ -183,7 +175,7 @@
 
     def dispatch(to, at, kind, sems):
         if kind == 2:
-            src, dst = esend.at[tile(to, 8)], erecv.at[tile(at, 8)]
+            src, dst = esend.at[to], erecv.at[at]
         else:
             src, dst = send.at[kind, tile(to, RANKS)], gbuf.at[y, kind, tile(at, RANKS)]
         return pltpu.make_async_remote_copy(
@@ -195,22 +187,25 @@
             device_id_type=MESH,
         )
 
-    def dispatch_x(off, carry):
-        to = lax.rem(f + off, frames)
+    def far_first(i):
+        return lax.rem(f + frames // 2 + (i + 1) // 2 * (1 - 2 * (i % 2)), frames)
+
+    def dispatch_x(i, carry):
+        to = far_first(i)
         dispatch(to, f, 0, to).start()
         dispatch(to, f, 2, to).start()
         return carry
 
-    def dispatch_g(off, carry):
-        to = lax.rem(f + off, frames)
+    def dispatch_g(i, carry):
+        to = far_first(i)
         dispatch(to, f, 1, to).start()
         return carry
 
-    lax.fori_loop(1, frames, dispatch_x, 0)
-    lax.fori_loop(1, frames, dispatch_g, 0)
+    lax.fori_loop(0, frames - 1, dispatch_x, 0)
+    lax.fori_loop(0, frames - 1, dispatch_g, 0)
     for kind in range(2):
         gbuf[y, kind, tile(f, RANKS), :] = send[kind, tile(f, RANKS), :]
-    erecv[tile(f, 8), :] = esend[tile(f, 8), :]
+    erecv[f] = esend[f]
 
     def arrived(kinds):
         def step(off, carry):
@@ -222,7 +217,7 @@
         lax.fori_loop(1, frames, step, 0)
 
     def unpack_extra(kind):
-        pieces = [erecv[pl.ds(2 * kind + j, frames, stride=8), :] for j in range(2)]
+        pieces = [erecv[:, 2 * kind + j, :] for j in range(2)]
         value = jnp.concatenate(pieces, axis=1)
         if slots - main > frames:
             value = jnp.concatenate(
@@ -304,7 +299,9 @@
 
     lax.fori_loop(0, slots // 16, hidden, 0)
 
-    parts = (slice(0, split), slice(split, slots))
+    edges = (0, split // 32 * 16, split, split + (slots - split) // 32 * 16, slots)
+    parts = tuple(slice(a, b) for a, b in zip(edges[:-1], edges[1:]))
+    groups = ((0, 1), (2, 3))
 
     def make_term(owner):
         at = columns(owner)
@@ -321,24 +318,25 @@
         )
 
     term[0] = make_term(lax.rem(y + half, experts))
-    for way in range(2):
-        rs_send[way, 0, parts[way]] = term[0, parts[way]].astype(BF16)
-        reduce_copy(way, 0, way).start()
+    for i in range(2):
+        for way in range(2):
+            part = groups[way][i]
+            rs_send[way, 0, parts[part]] = term[0, parts[part]].astype(BF16)
+            reduce_copy(way, 0, part).start()
 
     def reduce_step(step):
         for way in range(2):
             term[way] = make_term(
                 lax.rem(y + (half - step if way == 0 else experts - half + step), experts)
             )
-        for late in range(2):
-            for way in range(2):
-                part = way if late else 1 - way
-                value = term[way, parts[part]]
-                if late or not (isinstance(step, int) and step == 1):
-                    reduce_copy(way, step - 1, part).wait_recv()
-                    value = value + rs_recv[way, step - 1, parts[part]].astype(F32)
-                rs_send[way, step, parts[part]] = value.astype(BF16)
-                reduce_copy(way, step, part).start()
+        for late, i, way in [(l, i, w) for l in range(2) for i in range(2) for w in range(2)]:
+            part = groups[way if late else 1 - way][i]
+            value = term[way, parts[part]]
+            if late or not (isinstance(step, int) and step == 1):
+                reduce_copy(way, step - 1, part).wait_recv()
+                value = value + rs_recv[way, step - 1, parts[part]].astype(F32)
+            rs_send[way, step, parts[part]] = value.astype(BF16)
+            reduce_copy(way, step, part).start()
 
     reduce_step(1)
     if half > 2:
@@ -349,7 +347,7 @@
 
         lax.fori_loop(2, half, reduce_loop, 0)
     term[0] = make_term(y)
-    for part in range(2):
+    for part in range(4):
         for way in range(2):
             reduce_copy(way, half - 1, part).wait_recv()
         term[1, parts[part]] = (
@@ -360,29 +358,31 @@
     bsend[...] = term[1, 0:main].astype(BF16)
     back_extra = term[1, main:slots].astype(BF16).astype(F32)
     for j in range(2):
-        besend[pl.ds(j, frames, stride=8), :] = back_extra[:frames, j * LANE : (j + 1) * LANE]
+        besend[:, j, :] = back_extra[:frames, j * LANE : (j + 1) * LANE]
 
     def give_back(to, at, kind, sems):
-        size = (RANKS, 8)[kind]
-        src, dst = ((bsend, bk), (besend, berecv))[kind]
+        if kind == 0:
+            src, dst = bsend.at[tile(to, RANKS)], bk.at[tile(at, RANKS)]
+        else:
+            src, dst = besend.at[to], berecv.at[at]
         return pltpu.make_async_remote_copy(
-            src_ref=src.at[tile(to, size)],
-            dst_ref=dst.at[tile(at, size)],
+            src_ref=src,
+            dst_ref=dst,
             send_sem=bs_sem.at[kind, sems],
             recv_sem=br_sem.at[kind, at],
             device_id={"frame": to},
             device_id_type=MESH,
         )
 
-    def give_step(off, carry):
-        to = lax.rem(f + off, frames)
+    def give_step(i, carry):
+        to = far_first(i)
         for kind in range(2):
             give_back(to, f, kind, to).start()
         return carry
 
-    lax.fori_loop(1, frames, give_step, 0)
+    lax.fori_loop(0, frames - 1, give_step, 0)
     bk[tile(f, RANKS), :] = bsend[tile(f, RANKS), :]
-    berecv[tile(f, 8), :] = besend[tile(f, 8), :]
+    berecv[f] = besend[f]
     for load in loads[7:]:
         load.wait()
 
@@ -405,14 +405,14 @@
         return carry
 
     lax.fori_loop(1, frames, take_step, 0)
-    pieces = [berecv[pl.ds(j, frames, stride=8), :] for j in range(2)]
+    pieces = [berecv[:, j, :] for j in range(2)]
     returned_extra = jnp.concatenate(pieces, axis=1).astype(BF16)
     total = (
         og[...].astype(F32)
         + dot_tn(pt[0:main, :], bk[...])
         + dot_tn(pt[main : main + frames, :], returned_extra)
     )
-    igv[...] = total
+    totv[...] = total
     wbuf[1, 8 : 8 + tokens, :] = mo[...] * total
 
     inner = pl.ds(8, tokens)
@@ -435,9 +435,6 @@
     def _():
         frame_copy(1).start()
 
-    mgv[...] = total * co[...].astype(F32)
-    mg_out = pltpu.make_async_copy(mgv, mg_hbm, out_sem.at[0])
-    mg_out.start()
 
     chunk = 32
 
@@ -452,7 +449,7 @@
     places = (0, None, 1)
     for at in range(0, tokens, chunk):
         here = slice(at, at + chunk)
-        igv[here, :] += spread(1, 1, at)
+        convv[here, :] = spread(1, 1, at)
         for b in (0, 2):
             usend[places[b], here, :] = spread(b, 1, at)
 
@@ -488,20 +485,18 @@
         row_copy(1).start()
 
     for at in range(0, tokens, chunk):
-        igv[at : at + chunk, :] += spread(1, 0, at) + spread(1, 2, at)
+        convv[at : at + chunk, :] += spread(1, 0, at) + spread(1, 2, at)
 
     @pl.when(r < rows - 1)
     def _():
         row_copy(0).wait_recv()
-        igv[...] += urecv[0]
+        convv[...] += urecv[0]
 
     @pl.when(r > 0)
     def _():
         row_copy(1).wait_recv()
-        igv[...] += urecv[1]
-
-    ig_out = pltpu.make_async_copy(igv, ig_hbm, out_sem.at[1])
-    ig_out.start()
+        convv[...] += urecv[1]
+
 
     def sent(off, carry):
         to = lax.rem(f + off, frames)
@@ -518,8 +513,8 @@
                 if dist < half - 1 or kind == way:
                     gather(way, dist, kind).wait_send()
         for step in range(half):
-            for part in range(2):
-                if step > 0 or part == way:
+            for part in range(4):
+                if step > 0 or part in groups[way]:
                     reduce_copy(way, step, part).wait_send()
 
     @pl.when(f < frames - 1)
@@ -537,9 +532,6 @@
     @pl.when(r < rows - 1)
     def _():
         row_copy(1).wait_send()
-
-    mg_out.wait()
-    ig_out.wait()
 
 
 def shards(
@@ -557,7 +549,6 @@
     dma = pltpu.SemaphoreType.DMA
     scratch = [
         vmem((tokens, chan), BF16),
-        vmem((tokens, chan), BF16),
         vmem((tokens, chan), F32),
         vmem((3, 3, 3, chan), F32),
         vmem((tokens, chan), BF16),
@@ -566,11 +557,11 @@
         vmem((width, hidden), BF16),
         vmem((width, hidden), BF16),
         vmem((hidden, width), BF16),
-        dma((10,)),
+        dma((9,)),
         vmem((slots, tokens), BF16),
         vmem((2, main, chan), BF16),
-        vmem((frames * 8, LANE), F32),
-        vmem((frames * 8, LANE), F32),
+        vmem((frames, 4, LANE), F32),
+        vmem((frames, 4, LANE), F32),
         vmem((experts, 2, slots, chan), BF16),
         vmem((slots, hidden), F32),
         vmem((slots, hidden), F32),
@@ -581,21 +572,18 @@
         vmem((2, half, slots, chan), BF16),
         vmem((2, half, slots, chan), BF16),
         vmem((main, chan), BF16),
-        vmem((frames * 8, LANE), F32),
+        vmem((frames, 2, LANE), F32),
         vmem((main, chan), BF16),
-        vmem((frames * 8, LANE), F32),
+        vmem((frames, 2, LANE), F32),
         vmem((3, tokens + 16, chan), F32),
         vmem((2, tokens, chan), F32),
         vmem((2, tokens, chan), F32),
-        vmem((tokens, chan), F32),
-        vmem((tokens, chan), F32),
-        dma((2,)),
         dma((3, frames)),
         dma((3, frames)),
         dma((2, half, 2)),
         dma((2, half, 2)),
-        dma((2, half, 2)),
-        dma((2, half, 2)),
+        dma((2, half, 4)),
+        dma((2, half, 4)),
         dma((2, frames)),
         dma((2, frames)),
         dma((2,)),
@@ -603,16 +591,16 @@
         dma((2,)),
         dma((2,)),
     ]
-    out = jax.ShapeDtypeStruct((tokens, chan), F32)
+    out = pltpu.VMEM((tokens, chan), F32)
     slot_flops = 2 * slots * width * hidden
-    input_grad, mod_grad = pl.pallas_call(
+    total, spread = pl.pallas_call(
         functools.partial(body, frames, rows, experts, split),
         out_shape=(out, out),
-        in_specs=[pl.BlockSpec(memory_space=pl.ANY)] * 10,
-        out_specs=(pl.BlockSpec(memory_space=pl.ANY),) * 2,
+        in_specs=[pl.BlockSpec(memory_space=pl.ANY)] * 9,
+        out_specs=(pl.BlockSpec(memory_space=pltpu.VMEM),) * 2,
         scratch_shapes=scratch,
         compiler_params=pltpu.CompilerParams(
-            collective_id=0, has_side_effects=True, vmem_limit_bytes=60 * 2**20
+            collective_id=0, has_side_effects=True, vmem_limit_bytes=54 * 2**20
         ),
         cost_estimate=pl.CostEstimate(
             flops=5 * slot_flops,
@@ -622,7 +610,6 @@
         name="expert_backward",
     )(
         layer_input.reshape(tokens, chan),
-        conv_out.reshape(tokens, chan),
         modulation.reshape(tokens, chan),
         kernel,
         out_grad.reshape(tokens, chan),
@@ -632,8 +619,8 @@
         w_up.reshape(width, hidden),
         w_down.reshape(hidden, width),
     )
-    shape = (1, 1, tokens, chan)
-    return input_grad.reshape(shape), mod_grad.reshape(shape)
+    total, spread = (array.reshape(layer_input.shape) for array in (total, spread))
+    return total + spread, total * conv_out.astype(F32)
 
 
 def solution(mesh):

time: 90.1 us -> 85.6 us (0.950)
  local copies, waits for them, and re-layouts: 3.14 us -> 0.01 us
  Pallas kernels: 85.7 us -> 83.5 us
  other arithmetic: 0 us -> 1.34 us
    unnamed x2, local copies, waits for them, and re-layouts: 3.14 us -> 0.01 us
    pallas_call x1, Pallas kernels: 85.7 us -> 83.5 us  [shards(): pl.pallas_call(functools.partial(body, frames, rows, experts, split), out...]
where the time goes in v2:
time: 85.6 us; the launch traced here: 85.5 us
  Pallas kernels  83.5 us (98%)
  other arithmetic  1.34 us (2%)
    pallas_call x1, Pallas kernels, shards(): pl.pallas_call(functools.partial(body, frames, rows, experts, split), out...  83.5 us

profile of v2, /device:TPU:1, one launch (start us, length us, event | category | flops | bytes accessed | tf_op | source)
XLA Modules:
  0.0 85.5 jit_solution(2730042864355756333)
XLA Ops:
  0.6 0.0 copy-start
  0.6 83.5 %expert_backward.1 = (f32[128,256]{1,0:T(8,128)S(1)}, f32[128,256]{1,0:T(8,128)S(1)}) custom-call(bf16[128,256]{1,0:T(8,128)(2,1)} %bitcast.20, f32[128,256]{1,0:T(8,128)} %bitcast.19, f32[3,3,3,256]{3,2,1,0:T(4,128)} %ke_hbm.1, bf16[128,256]{1,0:T(8,128)(2,1)} %bitcast.21, s32[2,128]{1,0:T(2,128)} %bitcast.22, f32[2,128]{1,0:T(2,128)} %bitcast.23, ...), custom_call_target="tpu_custom_call" | custom-call | flops 4278190080 | bytes 9437184 | tf_op jit(solution)/shard_map/expert_backward/pallas_call | solution.py:596
  84.1 0.7 add_bitcast_fusion
  84.8 0.0 copy-done
  84.8 0.7 bitcast_multiply_fusion
Async XLA Ops:
  0.6 84.2 %copy-start = (bf16[1,1,128,256]{3,2,1,0:T(8,128)(2,1)S(1)}, bf16[1,1,128,256]{3,2,1,0:T(8,128)(2,1)}, u32[]{:S(2)}) copy-start(bf16[1,1,128,256]{3,2,1,0:T(8,128)(2,1)} %param.11) | copy-start | bytes 196612

commit v3 on v2

--- a/solution.py
+++ b/solution.py
@@ -37,7 +37,6 @@
     frames,
     rows,
     experts,
-    split,
     li_hbm,
     mo_hbm,
     ke_hbm,
@@ -77,6 +76,7 @@
     bk,
     berecv,
     wbuf,
+    uacc,
     usend,
     urecv,
     xs_sem,
@@ -170,51 +170,62 @@
 
     pl.semaphore_wait(barrier, frames - 1 + 2 + 2)
 
+    base = f - lax.rem(f, 2)
+    mid = main // 2
+    spans = (slice(0, mid), slice(mid, slots))
+    everything = slice(0, slots)
+    to_near, to_far = base + 4 + frames // 2, base + 4
+    from_near, from_far = base - 2 + frames, base - 2 + frames + frames // 2
+
     def tile(index, size):
         return pl.ds(pl.multiple_of(index * size, size), size)
 
-    def dispatch(to, at, kind, sems):
+    def place(source, expert):
+        return lax.rem(source - (expert - lax.rem(expert, 2)) + 2 + frames, frames)
+
+    def others(first, kinds, act):
+        def step(j, carry):
+            peer = lax.rem(first + j, frames)
+
+            @pl.when(peer != f)
+            def _():
+                for kind in kinds:
+                    act(peer, kind)
+
+            return carry
+
+        lax.fori_loop(0, frames // 2, step, 0)
+
+    def dispatch(peer, kind, sending):
+        source, expert = (f, peer) if sending else (peer, f)
         if kind == 2:
-            src, dst = esend.at[to], erecv.at[at]
+            src, dst = esend.at[peer], erecv.at[source]
         else:
-            src, dst = send.at[kind, tile(to, RANKS)], gbuf.at[y, kind, tile(at, RANKS)]
+            src = send.at[kind, tile(peer, RANKS)]
+            dst = gbuf.at[y, kind, tile(place(source, expert), RANKS)]
         return pltpu.make_async_remote_copy(
             src_ref=src,
             dst_ref=dst,
-            send_sem=xs_sem.at[kind, sems],
-            recv_sem=xr_sem.at[kind, at],
-            device_id={"frame": to},
+            send_sem=xs_sem.at[kind, peer],
+            recv_sem=xr_sem.at[kind, source],
+            device_id={"frame": peer},
             device_id_type=MESH,
         )
 
-    def far_first(i):
-        return lax.rem(f + frames // 2 + (i + 1) // 2 * (1 - 2 * (i % 2)), frames)
-
-    def dispatch_x(i, carry):
-        to = far_first(i)
-        dispatch(to, f, 0, to).start()
-        dispatch(to, f, 2, to).start()
-        return carry
-
-    def dispatch_g(i, carry):
-        to = far_first(i)
-        dispatch(to, f, 1, to).start()
-        return carry
-
-    lax.fori_loop(0, frames - 1, dispatch_x, 0)
-    lax.fori_loop(0, frames - 1, dispatch_g, 0)
+    def dispatch_start(peer, kind):
+        dispatch(peer, kind, True).start()
+
+    def dispatch_wait(peer, kind):
+        dispatch(peer, kind, False).wait_recv()
+
+    others(to_near, (0,), dispatch_start)
+    others(to_near, (1,), dispatch_start)
+    others(to_far, (0, 2), dispatch_start)
+    others(to_near, (2,), dispatch_start)
+    others(to_far, (1,), dispatch_start)
     for kind in range(2):
-        gbuf[y, kind, tile(f, RANKS), :] = send[kind, tile(f, RANKS), :]
+        gbuf[y, kind, tile(place(f, f), RANKS), :] = send[kind, tile(f, RANKS), :]
     erecv[f] = esend[f]
-
-    def arrived(kinds):
-        def step(off, carry):
-            at = lax.rem(f + off, frames)
-            for kind in kinds:
-                dispatch(at, at, kind, at).wait_recv()
-            return carry
-
-        lax.fori_loop(1, frames, step, 0)
 
     def unpack_extra(kind):
         pieces = [erecv[:, 2 * kind + j, :] for j in range(2)]
@@ -225,13 +236,16 @@
             )
         gbuf[y, kind, main:slots, :] = value.astype(BF16)
 
-    def gather(way, dist, kind):
-        owner = lax.rem(y + (experts - dist if way == 0 else dist), experts)
+    def owner_of(way, dist):
+        return lax.rem(y + (experts - dist if way == 0 else dist), experts)
+
+    def gather(way, dist, kind, span):
+        ref = gbuf.at[owner_of(way, dist), kind, spans[span]]
         return pltpu.make_async_remote_copy(
-            src_ref=gbuf.at[owner, kind],
-            dst_ref=gbuf.at[owner, kind],
-            send_sem=as_sem.at[way, dist, kind],
-            recv_sem=ar_sem.at[way, dist, kind],
+            src_ref=ref,
+            dst_ref=ref,
+            send_sem=as_sem.at[way, dist, kind, span],
+            recv_sem=ar_sem.at[way, dist, kind, span],
             device_id={"expert": right if way == 0 else left},
             device_id_type=MESH,
         )
@@ -239,73 +253,52 @@
     def columns(owner):
         return pl.ds(pl.multiple_of(owner * chan, chan), chan)
 
-    def add_block(owner, kind, first):
-        block = gbuf[owner, kind]
+    def add_block(owner, kind, span, first=False):
+        rows_of = everything if span is None else spans[span]
+        block = gbuf[owner, kind, rows_of]
         for n in range(0, hg.shape[1], chan):
             cut = slice(n, n + chan)
             if kind == 0:
                 for acc, w in ((hg, wg), (hu, wu)):
                     value = dot_nn(block, w[columns(owner), cut])
-                    acc[:, cut] = value if first else acc[:, cut] + value
+                    acc[rows_of, cut] = value if first else acc[rows_of, cut] + value
             else:
                 value = dot_nt(block, wd[cut, columns(owner)])
-                ag[:, cut] = value if first else ag[:, cut] + value
-
-    arrived((0, 2))
-    unpack_extra(0)
-    for way in range(2):
-        gather(way, 0, 0).start()
-    loads[4].wait()
-    loads[5].wait()
-    add_block(y, 0, True)
-    arrived((1,))
-    unpack_extra(1)
-    for way in range(2):
-        gather(way, 0, 1).start()
-    loads[6].wait()
-    add_block(y, 1, True)
-
-    def owner_of(way, dist):
-        return lax.rem(y + (experts - dist if way == 0 else dist), experts)
-
-    def ring(dist):
-        for kind in range(2):
-            for way in range(2):
-                gather(way, dist - 1, kind).wait_recv()
-                if isinstance(dist, int) and dist == half - 1:
-                    if kind == way:
-                        gather(way, dist, kind).start()
-                else:
-                    gather(way, dist, kind).start()
-            for way in range(2):
-                add_block(owner_of(way, dist), kind, False)
-
-    if half > 2:
-
-        def ring_step(dist, carry):
-            ring(dist)
+                ag[rows_of, cut] = value if first else ag[rows_of, cut] + value
+
+    def gather_own(kind, span):
+        for way in range(2):
+            gather(way, 0, kind, span).start()
+
+    def forward(dist, kind, span):
+        for way in range(2):
+            gather(way, dist - 1, kind, span).wait_recv()
+            if dist < half - 1 or kind == way:
+                gather(way, dist, kind, span).start()
+
+    def compute(dist, kind, span):
+        for way in range(2):
+            add_block(owner_of(way, dist), kind, span)
+
+    def ring_last(span):
+        for way in range(2):
+            gather(way, half - 1, way, span).wait_recv()
+            add_block(owner_of(way, half), way, span)
+
+    def hidden(span):
+        def step(i, carry):
+            at = tile(i, 16)
+            gg[at, :], ug[at, :] = hidden_grads(hg[at, :], hu[at, :], ag[at, :])
             return carry
 
-        lax.fori_loop(1, half - 1, ring_step, 0)
-    ring(half - 1)
-    for way in range(2):
-        gather(way, half - 1, way).wait_recv()
-        add_block(owner_of(way, half), way, False)
-
-    def hidden(i, carry):
-        at = tile(i, 16)
-        gg[at, :], ug[at, :] = hidden_grads(hg[at, :], hu[at, :], ag[at, :])
-        return carry
-
-    lax.fori_loop(0, slots // 16, hidden, 0)
-
-    edges = (0, split // 32 * 16, split, split + (slots - split) // 32 * 16, slots)
+        lax.fori_loop(spans[span].start // 16, spans[span].stop // 16, step, 0)
+
+    edges = (0, mid // 32 * 16, mid, mid + ((slots - mid) // 16 + 1) // 2 * 16, slots)
     parts = tuple(slice(a, b) for a, b in zip(edges[:-1], edges[1:]))
-    groups = ((0, 1), (2, 3))
-
-    def make_term(owner):
-        at = columns(owner)
-        return dot_nt(gg[...], wg[at, :]) + dot_nt(ug[...], wu[at, :])
+
+    def make_term(owner, span):
+        at, rows_of = columns(owner), spans[span]
+        return dot_nt(gg[rows_of], wg[at, :]) + dot_nt(ug[rows_of], wu[at, :])
 
     def reduce_copy(way, step, part):
         return pltpu.make_async_remote_copy(
@@ -317,71 +310,110 @@
             device_id_type=MESH,
         )
 
-    term[0] = make_term(lax.rem(y + half, experts))
-    for i in range(2):
+    def reduce_first(span):
+        term[0, spans[span]] = make_term(lax.rem(y + half, experts), span)
         for way in range(2):
-            part = groups[way][i]
+            part = 2 * span + way
             rs_send[way, 0, parts[part]] = term[0, parts[part]].astype(BF16)
             reduce_copy(way, 0, part).start()
 
-    def reduce_step(step):
+    def reduce_step(step, span):
         for way in range(2):
-            term[way] = make_term(
-                lax.rem(y + (half - step if way == 0 else experts - half + step), experts)
+            term[way, spans[span]] = make_term(
+                lax.rem(y + (half - step if way == 0 else experts - half + step), experts), span
             )
-        for late, i, way in [(l, i, w) for l in range(2) for i in range(2) for w in range(2)]:
-            part = groups[way if late else 1 - way][i]
+        for late, way in ((0, 0), (0, 1), (1, 0), (1, 1)):
+            part = 2 * span + (way if late else 1 - way)
             value = term[way, parts[part]]
-            if late or not (isinstance(step, int) and step == 1):
+            if late or step > 1:
                 reduce_copy(way, step - 1, part).wait_recv()
                 value = value + rs_recv[way, step - 1, parts[part]].astype(F32)
             rs_send[way, step, parts[part]] = value.astype(BF16)
             reduce_copy(way, step, part).start()
 
-    reduce_step(1)
-    if half > 2:
-
-        def reduce_loop(step, carry):
-            reduce_step(step)
-            return carry
-
-        lax.fori_loop(2, half, reduce_loop, 0)
-    term[0] = make_term(y)
-    for part in range(4):
-        for way in range(2):
-            reduce_copy(way, half - 1, part).wait_recv()
-        term[1, parts[part]] = (
-            term[0, parts[part]]
-            + rs_recv[0, half - 1, parts[part]].astype(F32)
-            + rs_recv[1, half - 1, parts[part]].astype(F32)
-        )
-    bsend[...] = term[1, 0:main].astype(BF16)
-    back_extra = term[1, main:slots].astype(BF16).astype(F32)
-    for j in range(2):
-        besend[:, j, :] = back_extra[:frames, j * LANE : (j + 1) * LANE]
-
-    def give_back(to, at, kind, sems):
+    def give_back(peer, kind, sending):
+        expert = f if sending else peer
         if kind == 0:
-            src, dst = bsend.at[tile(to, RANKS)], bk.at[tile(at, RANKS)]
+            src, dst = bsend.at[tile(place(peer, f), RANKS)], bk.at[tile(expert, RANKS)]
         else:
-            src, dst = besend.at[to], berecv.at[at]
+            src, dst = besend.at[peer], berecv.at[expert]
         return pltpu.make_async_remote_copy(
             src_ref=src,
             dst_ref=dst,
-            send_sem=bs_sem.at[kind, sems],
-            recv_sem=br_sem.at[kind, at],
-            device_id={"frame": to},
+            send_sem=bs_sem.at[kind, peer],
+            recv_sem=br_sem.at[kind, expert],
+            device_id={"frame": peer},
             device_id_type=MESH,
         )
 
-    def give_step(i, carry):
-        to = far_first(i)
+    def give_start(peer, kind):
+        give_back(peer, kind, True).start()
+
+    def give_wait(peer, kind):
+        give_back(peer, kind, False).wait_recv()
+
+    def reduce_last(span):
+        term[0, spans[span]] = make_term(y, span)
+        for part in (2 * span, 2 * span + 1):
+            for way in range(2):
+                reduce_copy(way, half - 1, part).wait_recv()
+            term[1, parts[part]] = (
+                term[0, parts[part]]
+                + rs_recv[0, half - 1, parts[part]].astype(F32)
+                + rs_recv[1, half - 1, parts[part]].astype(F32)
+            )
+        if span == 0:
+            bsend[0:mid] = term[1, 0:mid].astype(BF16)
+            others(from_near, (0,), give_start)
+        else:
+            bsend[mid:main] = term[1, mid:main].astype(BF16)
+            others(from_far, (0,), give_start)
+            back_extra = term[1, main:slots].astype(BF16).astype(F32)
+            for j in range(2):
+                besend[:, j, :] = back_extra[:frames, j * LANE : (j + 1) * LANE]
+            others(from_far, (1,), give_start)
+            others(from_near, (1,), give_start)
+
+    others(from_near, (0,), dispatch_wait)
+    gather_own(0, 0)
+    others(from_near, (1,), dispatch_wait)
+    gather_own(1, 0)
+    others(from_far, (0, 2), dispatch_wait)
+    others(from_near, (2,), dispatch_wait)
+    unpack_extra(0)
+    gather_own(0, 1)
+    for kind in range(2):
+        forward(1, kind, 0)
+    others(from_far, (1,), dispatch_wait)
+    unpack_extra(1)
+    gather_own(1, 1)
+    for load in loads[4:7]:
+        load.wait()
+    for kind in range(2):
+        add_block(y, kind, None, True)
+    for dist in range(2, half):
         for kind in range(2):
-            give_back(to, f, kind, to).start()
-        return carry
-
-    lax.fori_loop(0, frames - 1, give_step, 0)
-    bk[tile(f, RANKS), :] = bsend[tile(f, RANKS), :]
+            forward(dist, kind, 0)
+        for kind in range(2):
+            forward(dist - 1, kind, 1)
+            compute(dist - 1, kind, None)
+    for kind in range(2):
+        compute(half - 1, kind, 0)
+        forward(half - 1, kind, 1)
+    ring_last(0)
+    hidden(0)
+    reduce_first(0)
+    for kind in range(2):
+        compute(half - 1, kind, 1)
+    ring_last(1)
+    hidden(1)
+    reduce_first(1)
+    for step in range(1, half):
+        reduce_step(step, 0)
+        reduce_step(step, 1)
+    reduce_last(0)
+    reduce_last(1)
+    bk[tile(f, RANKS), :] = bsend[tile(place(f, f), RANKS), :]
     berecv[f] = besend[f]
     for load in loads[7:]:
         load.wait()
@@ -398,13 +430,8 @@
     def _():
         wbuf[2, 8 : 8 + tokens, :] = jnp.zeros((tokens, chan), F32)
 
-    def take_step(off, carry):
-        at = lax.rem(f + off, frames)
-        for kind in range(2):
-            give_back(at, at, kind, at).wait_recv()
-        return carry
-
-    lax.fori_loop(1, frames, take_step, 0)
+    others(from_near, (0, 1), give_wait)
+    others(from_far, (0, 1), give_wait)
     pieces = [berecv[:, j, :] for j in range(2)]
     returned_extra = jnp.concatenate(pieces, axis=1).astype(BF16)
     total = (
@@ -451,7 +478,7 @@
         here = slice(at, at + chunk)
         convv[here, :] = spread(1, 1, at)
         for b in (0, 2):
-            usend[places[b], here, :] = spread(b, 1, at)
+            uacc[places[b], here, :] = spread(b, 1, at)
 
     @pl.when(f > 0)
     def _():
@@ -460,11 +487,6 @@
     @pl.when(f < frames - 1)
     def _():
         frame_copy(1).wait_recv()
-
-    for b in (0, 2):
-        for at in range(0, tokens, chunk):
-            here = slice(at, at + chunk)
-            usend[places[b], here, :] += spread(b, 0, at) + spread(b, 2, at)
 
     def row_copy(way):
         return pltpu.make_async_remote_copy(
@@ -476,9 +498,19 @@
             device_id_type=MESH,
         )
 
+    def add_frames(b):
+        for at in range(0, tokens, chunk):
+            here = slice(at, at + chunk)
+            value = uacc[places[b], here, :] + spread(b, 0, at) + spread(b, 2, at)
+            usend[places[b], here, :] = value.astype(BF16)
+
+    add_frames(0)
+
     @pl.when(r > 0)
     def _():
         row_copy(0).start()
+
+    add_frames(2)
 
     @pl.when(r < rows - 1)
     def _():
@@ -490,32 +522,27 @@
     @pl.when(r < rows - 1)
     def _():
         row_copy(0).wait_recv()
-        convv[...] += urecv[0]
+        convv[...] += urecv[0].astype(F32)
 
     @pl.when(r > 0)
     def _():
         row_copy(1).wait_recv()
-        convv[...] += urecv[1]
-
-
-    def sent(off, carry):
-        to = lax.rem(f + off, frames)
-        for kind in range(3):
-            dispatch(to, f, kind, to).wait_send()
-        for kind in range(2):
-            give_back(to, f, kind, to).wait_send()
-        return carry
-
-    lax.fori_loop(1, frames, sent, 0)
+        convv[...] += urecv[1].astype(F32)
+
+
+    for first in (from_near, from_far):
+        others(first, (0, 1, 2), lambda peer, kind: dispatch(peer, kind, True).wait_send())
+        others(first, (0, 1), lambda peer, kind: give_back(peer, kind, True).wait_send())
     for way in range(2):
-        for dist in range(half):
-            for kind in range(2):
-                if dist < half - 1 or kind == way:
-                    gather(way, dist, kind).wait_send()
-        for step in range(half):
-            for part in range(4):
-                if step > 0 or part in groups[way]:
-                    reduce_copy(way, step, part).wait_send()
+        for span in range(2):
+            for dist in range(half):
+                for kind in range(2):
+                    if dist < half - 1 or kind == way:
+                        gather(way, dist, kind, span).wait_send()
+            for step in range(half):
+                for part in (2 * span, 2 * span + 1):
+                    if step > 0 or part == 2 * span + way:
+                        reduce_copy(way, step, part).wait_send()
 
     @pl.when(f < frames - 1)
     def _():
@@ -543,7 +570,6 @@
     assert w_gate.shape[0] == 1 and 2 * tokens == RANKS * frames and chan == 2 * LANE
     main = frames * RANKS
     slots = main + -(-frames // 16) * 16
-    split = (slots // 16 + 1) // 2 * 16
     half = experts // 2
     vmem = pltpu.VMEM
     dma = pltpu.SemaphoreType.DMA
@@ -577,11 +603,12 @@
         vmem((frames, 2, LANE), F32),
         vmem((3, tokens + 16, chan), F32),
         vmem((2, tokens, chan), F32),
-        vmem((2, tokens, chan), F32),
+        vmem((2, tokens, chan), BF16),
+        vmem((2, tokens, chan), BF16),
         dma((3, frames)),
         dma((3, frames)),
-        dma((2, half, 2)),
-        dma((2, half, 2)),
+        dma((2, half, 2, 2)),
+        dma((2, half, 2, 2)),
         dma((2, half, 4)),
         dma((2, half, 4)),
         dma((2, frames)),
@@ -594,7 +621,7 @@
     out = pltpu.VMEM((tokens, chan), F32)
     slot_flops = 2 * slots * width * hidden
     total, spread = pl.pallas_call(
-        functools.partial(body, frames, rows, experts, split),
+        functools.partial(body, frames, rows, experts),
         out_shape=(out, out),
         in_specs=[pl.BlockSpec(memory_space=pl.ANY)] * 9,
         out_specs=(pl.BlockSpec(memory_space=pltpu.VMEM),) * 2,

time: 85.6 us -> 83.8 us (0.979)
  Pallas kernels: 83.5 us -> 81.7 us
    pallas_call x1, Pallas kernels: 83.5 us -> 81.7 us  [shards(): pl.pallas_call(functools.partial(body, frames, rows, experts), out_shape=...]
where the time goes in v3:
time: 83.8 us; the launch traced here: 83.7 us
  Pallas kernels  81.7 us (97%)
  other arithmetic  1.34 us (2%)
    pallas_call x1, Pallas kernels, shards(): pl.pallas_call(functools.partial(body, frames, rows, experts), out_shape=...  81.7 us

profile of v3, /device:TPU:1, one launch (start us, length us, event | category | flops | bytes accessed | tf_op | source)
XLA Modules:
  0.0 83.7 jit_solution(8775600164031425531)
XLA Ops:
  0.6 0.0 copy-start
  0.6 81.7 %expert_backward.1 = (f32[128,256]{1,0:T(8,128)S(1)}, f32[128,256]{1,0:T(8,128)S(1)}) custom-call(bf16[128,256]{1,0:T(8,128)(2,1)} %bitcast.20, f32[128,256]{1,0:T(8,128)} %bitcast.19, f32[3,3,3,256]{3,2,1,0:T(4,128)} %ke_hbm.1, bf16[128,256]{1,0:T(8,128)(2,1)} %bitcast.21, s32[2,128]{1,0:T(2,128)} %bitcast.22, f32[2,128]{1,0:T(2,128)} %bitcast.23, ...), custom_call_target="tpu_custom_call" | custom-call | flops 4278190080 | bytes 9437184 | tf_op jit(solution)/shard_map/expert_backward/pallas_call | solution.py:623
  82.3 0.7 add_bitcast_fusion
  83.0 0.0 copy-done
  83.0 0.7 bitcast_multiply_fusion
Async XLA Ops:
  0.6 82.4 %copy-start = (bf16[1,1,128,256]{3,2,1,0:T(8,128)(2,1)S(1)}, bf16[1,1,128,256]{3,2,1,0:T(8,128)(2,1)}, u32[]{:S(2)}) copy-start(bf16[1,1,128,256]{3,2,1,0:T(8,128)(2,1)} %param.11) | copy-start | bytes 196612
